TPU v7x, 32 devices: a whole 2x2x4 slice. The times are simulated.
32 devices in a mesh: groups: 2 (over y), zone: 4 (over z), scen: 2 (over x), hour: 2 (over core).
Axes of the slice: x: 2, y: 2, z: 4, core: 2. Of those that a mesh axis runs over, the one named last changes fastest.
Arguments:
- forcing: bfloat16 [1024, 48, 64], P(('groups', 'zone', 'scen', 'hour')), parts along dimension 0, may hold values from -3 to 3
- response: bfloat16 [48, 64, 8192], P('hour', None, ('groups', 'zone')), parts along dimension 2, may hold values from -0.75 to 0.75
- window_params: float32 [128, 64], P('groups'), parts along dimension 0, may hold values from 0.5 to 1.5
- building_map: int32 [8192], P(('groups', 'zone')), parts along dimension 0, may hold values from 0 to 1023
- owner_ids: int32 [2048], P('groups'), parts along dimension 0, may hold values from 0 to 63
- band_ids: int32 [48, 8192], P('hour', ('groups', 'zone')), parts along dimension 1, may hold values from 0 to 7
- floor_area: float32 [8192], P(('groups', 'zone')), parts along dimension 0, may hold values from 0.5 to 18, as said below
Outputs:
- sensitivity: float32 [128, 64], P(('groups', 'zone', 'scen', 'hour')), parts along dimension 0
- objective: float32 [2], P('groups'), parts along dimension 0
There are 2 independent parts, one for each index of `groups`. A program takes and returns all parts, laid end to end along the dimension named above; each array names one. Nothing has to cross between parts.
Inputs may be any that keep to these rules, and one draw needn't show every extreme that they name: `floor_area`: floor areas are positive.
All inputs are finite; a program needn't handle non-finite values.
Results may differ from a plain program's by a relative error of at most 0.0006.
Values may be sent and summed in bfloat16 or wider, within the bound.
A program may use at most 128 MiB of HBM per device.

v0:
```python
import math
import jax
import jax.numpy as jnp
from jax import lax
from jax.sharding import PartitionSpec as P

SHARPNESS = 200.0


def joined(value, axis, join):
    pieces = jax.tree.map(lambda part: lax.all_gather(part, axis), value)
    head = jax.tree.map(lambda part: part[0], pieces)
    tail = jax.tree.map(lambda part: part[1:], pieces)
    running, _ = lax.scan(lambda running, share: (join(running, share), None), head, tail)
    return running


def merge_softmax(first, second):
    highest = jnp.maximum(first[0], second[0])
    return (
        highest,
        first[1] * jnp.exp(first[0] - highest) + second[1] * jnp.exp(second[0] - highest),
    )


def on_device(forcing, response, window_params, building_map, owner_ids, band_ids, floor_area):
    hour_local = response.shape[0]
    width = response.shape[1]
    zone_local = response.shape[2]
    hours_total = hour_local * lax.axis_size("hour")
    hour_first = lax.axis_index("hour") * hour_local
    positions = (hour_first + jnp.arange(hour_local)).astype(jnp.float32)
    occupant_level = 1.0 + 2.0 * positions / (hours_total - 1)
    candidate_plan = jnp.take(owner_ids, building_map)
    zone_parameters = jnp.take(window_params, candidate_plan, axis=0)
    coeff = (response.astype(jnp.float32) * zone_parameters.T[None, :, :]).astype(jnp.bfloat16)
    band_low = 0.25 * (band_ids.astype(jnp.float32) - 3.5) - 0.5
    band_high = band_low + 1.0
    zone_weight = occupant_level[:, None] * floor_area[None, :]
    block_count = hour_local // 8
    mine = lax.all_to_all(forcing, "hour", split_axis=1, concat_axis=0, tiled=True)

    def inside_climate_state(outlook_records, initial_clock_time):
        record_elements = lax.slice_in_dim(
            outlook_records, initial_clock_time, initial_clock_time + 8, axis=1
        )
        thermal_demand = jnp.einsum(
            "shp,hpz->hsz",
            record_elements,
            coeff[initial_clock_time : initial_clock_time + 8],
            preferred_element_type=jnp.float32,
        )
        return (thermal_demand, record_elements)

    weight_part = (jnp.sum(floor_area) * jnp.sum(occupant_level)).reshape(1)
    outlook_records = lax.all_gather(mine, "zone", axis=0, tiled=True)
    sums = jnp.zeros((outlook_records.shape[0],), jnp.float32)
    for hour_block in range(block_count):
        initial_clock_time = hour_block * 8
        thermal_demand, record_elements = inside_climate_state(outlook_records, initial_clock_time)
        low = band_low[initial_clock_time : initial_clock_time + 8][:, None, :]
        high = band_high[initial_clock_time : initial_clock_time + 8][:, None, :]
        penalty = jax.nn.softplus(thermal_demand - high) + jax.nn.softplus(low - thermal_demand)
        sums = sums + jnp.sum(
            penalty * zone_weight[initial_clock_time : initial_clock_time + 8][:, None, :],
            axis=(0, 2),
        )
    loss_sum, weight_total = lax.psum((sums, weight_part), ("zone", "hour"))
    scores = SHARPNESS * loss_sum / weight_total[0]
    local_peak = jnp.max(scores)
    peak_score, exp_total = joined(
        (local_peak, jnp.sum(jnp.exp(scores - local_peak))), "scen", merge_softmax
    )
    objective = ((peak_score + jnp.log(exp_total)) / SHARPNESS).reshape(1)
    scen_weight = jnp.exp(scores - peak_score) / exp_total / weight_total[0]
    empty = jnp.zeros((width, zone_local), jnp.float32)
    accumulated = empty
    outlook_records = lax.all_gather(mine, "zone", axis=0, tiled=True)
    for hour_block in range(block_count):
        initial_clock_time = hour_block * 8
        thermal_demand, record_elements = inside_climate_state(outlook_records, initial_clock_time)
        low = band_low[initial_clock_time : initial_clock_time + 8][:, None, :]
        high = band_high[initial_clock_time : initial_clock_time + 8][:, None, :]
        slope = jax.nn.sigmoid(thermal_demand - high) - jax.nn.sigmoid(low - thermal_demand)
        adjoint = (
            slope
            * scen_weight[None, :, None]
            * zone_weight[initial_clock_time : initial_clock_time + 8][:, None, :]
        ).astype(jnp.bfloat16)
        mixed = jnp.einsum(
            "shp,hsz->hpz", record_elements, adjoint, preferred_element_type=jnp.float32
        )
        accumulated = accumulated + jnp.sum(
            response[initial_clock_time : initial_clock_time + 8].astype(jnp.float32) * mixed,
            axis=0,
        )
    zones_all = zone_local * lax.axis_size("zone")
    designs = window_params.shape[0]
    gain = math.sqrt(width * zones_all * hours_total * designs)
    zone_rows = accumulated.T
    owners_local = designs // (
        lax.axis_size("zone") * lax.axis_size("scen") * lax.axis_size("hour")
    )
    onehot = (
        candidate_plan[:, None]
        == jnp.arange(owners_local * lax.axis_size(("zone", "scen", "hour")))[None, :]
    ).astype(jnp.float32)
    sensitivity = lax.psum_scatter(
        gain * jnp.dot(onehot.T, zone_rows, precision=lax.Precision.HIGHEST),
        ("zone", "scen", "hour"),
        scatter_dimension=0,
        tiled=True,
    )
    return (sensitivity, objective)


def solution(mesh):
    in_specs = (
        P(("groups", "zone", "scen", "hour"), None, None),
        P("hour", None, ("groups", "zone")),
        P("groups", None),
        P(("groups", "zone")),
        P("groups"),
        P("hour", ("groups", "zone")),
        P(("groups", "zone")),
    )
    out_specs = (P(("groups", "zone", "scen", "hour"), None), P("groups"))
    return jax.shard_map(
        on_device, mesh=mesh, in_specs=in_specs, out_specs=out_specs, check_vma=False
    )
```

profile of v0, /device:TPU:0, one launch (start us, length us, event | category | flops | bytes accessed | tf_op | source)
XLA Modules:
  0.0 207.4 jit_solution(13071616913442641954)
XLA Ops:
  0.6 0.0 copy-start
  0.6 0.0 copy-start.3
  0.7 0.0 copy-start.2
  0.7 0.0 copy-start.4
  0.7 0.0 copy-start.1
  0.7 1.2 copy.37
  1.8 1.0 reshape.77
  2.9 3.4 %all-to-all-start = ((bf16[2,2,24576]{2,1,0:T(2,128)(2,1)}), bf16[2,2,24576]{2,1,0:T(2,128)(2,1)S(1)}, u32[]{:S(2)}, u32[]{:S(2)}) async-start(bf16[2,2,24576]{2,1,0:T(2,128)(2,1)} %reshape.77), calls=%async_computation | async-start | bytes 393216 | tf_op jit(solution)/shard_map/all_to_all | solution.py:41
  6.3 1.5 all-to-all-done
  7.8 0.3 reshape.78
  8.1 0.2 copy.22
  8.2 31.7 %all_gather.16 = bf16[256,24,64]{2,1,0:T(8,128)(2,1)S(1)} all-gather(bf16[64,24,64]{2,1,0:T(8,128)(2,1)S(1)} %bitcast.231), channel_id=1, replica_groups=mesh['groups'=2,'zone'=4,'scen'=2,'hour'=2] {'zone'}, dimensions={0}, use_global_device_ids=true | all-gather | bytes 983040 | tf_op jit(solution)/shard_map/all_gather | solution.py:78
  40.0 0.3 fusion.95
  40.2 0.3 copy.35
  40.6 0.6 multiply_add_fusion
  41.2 0.0 copy-done.3
  41.2 0.1 broadcast_multiply_fusion
  41.3 0.0 copy-done.2
  41.3 0.0 copy-done.4
  41.3 0.0 copy-done.1
  41.3 4.5 %gather_fusion = s32[1024]{0:T(1024)S(1)} fusion(s32[1024]{0:T(1024)S(1)} %copy-done.1, s32[1024]{0:T(1024)S(1)} %fusion.88), kind=kCustom, calls=%fused_computation | custom fusion | bytes 12288 | tf_op jit(solution)/shard_map/jit(_take)/gather | solution.py:34
  45.9 0.0 copy-done
  45.9 2.8 %gather_fusion.1 = f32[1024,64]{1,0:T(8,128)S(1)} fusion(f32[64,64]{1,0:T(8,128)S(1)} %copy-done, s32[1024]{0:T(1024)S(1)} %fusion.89), kind=kCustom, calls=%fused_computation.1 | custom fusion | bytes 528384 | tf_op jit(solution)/shard_map/jit(_take)/gather | solution.py:35
  48.7 0.2 select_bitcast_fusion
  48.9 0.2 copy.19
  49.1 0.3 copy.33
  49.5 0.3 copy.34
  49.8 0.6 reduce_sum.84
  51.7 0.0 copy-start.5
  51.7 13.8 %fusion.8 = (f32[256]{0:T(256)S(1)}, f32[8,1024,256]{2,1,0:T(8,128)}) fusion(f32[8,1024]{1,0:T(8,128)S(1)} %get-tuple-element.35, f32[8,1024]{1,0:T(8,128)S(1)} %get-tuple-element.52, f32[8,1024]{1,0:T(8,128)S(1)} %get-tuple-element.29, bf16[256,8,64]{0,2,1:T(8,128)(2,1)S(1)} %copy.35, bf16[24,64,1024]{2,1,0:T(8,128)(2,1)} %param.8, f32[64,1024]{1,0:T(8,128)S(1)} %copy.19), kind=kOutput, calls=%fused_computation.16 | convolution fusion | flops 308805376 | bytes 12157952 | tf_op jit(solution)/shard_map/shp,hpz->hsz/dot_general | solution.py:47
  65.5 0.0 copy-done.5
  65.5 13.3 %fusion.2 = (f32[256]{0:T(256)S(1)}, f32[8,1024,256]{2,1,0:T(8,128)}) fusion(f32[8,1024]{1,0:T(8,128)S(1)} %get-tuple-element.36, f32[8,1024]{1,0:T(8,128)S(1)} %get-tuple-element.51, f32[8,1024]{1,0:T(8,128)S(1)} %get-tuple-element.30, bf16[256,8,64]{0,2,1:T(8,128)(2,1)S(1)} %copy.33, bf16[24,64,1024]{2,1,0:T(8,128)(2,1)S(1)} %copy-done.5, ...), kind=kOutput, calls=%fused_computation.10 | convolution fusion | flops 308805376 | bytes 12157952 | tf_op jit(solution)/shard_map/shp,hpz->hsz/dot_general | solution.py:47
  78.8 0.0 copy-start.8
  78.8 13.2 %fusion.5 = (f32[256]{0:T(256)S(1)}, f32[8,1024,256]{2,1,0:T(8,128)}) fusion(f32[8,1024]{1,0:T(8,128)S(1)} %get-tuple-element.34, f32[8,1024]{1,0:T(8,128)S(1)} %get-tuple-element.53, f32[8,1024]{1,0:T(8,128)S(1)} %get-tuple-element.28, bf16[256,8,64]{0,2,1:T(8,128)(2,1)S(1)} %copy.34, bf16[24,64,1024]{2,1,0:T(8,128)(2,1)S(1)} %copy-done.5, ...), kind=kOutput, calls=%fused_computation.13 | convolution fusion | flops 308805376 | bytes 12157952 | tf_op jit(solution)/shard_map/shp,hpz->hsz/dot_general | solution.py:47
  92.0 16.5 %all-reduce.3 = (f32[256]{0:T(256)S(1)}, f32[]{:T(128)}) all-reduce(f32[256]{0:T(256)S(1)} %add_add_fusion, f32[]{:T(128)S(6)} %mul.142), channel_id=1, replica_groups=mesh['groups'=2,'zone'=4,'scen'=2,'hour'=2] {'zone','hour'}, use_global_device_ids=true, to_apply=%region_3.4 | all-reduce | flops 257 | bytes 2056 | tf_op jit(solution)/shard_map/psum | solution.py:68
  108.5 1.2 fusion.94
  109.8 1.3 exponential_reduce_fusion
  111.0 0.0 copy-done.8
  111.0 0.6 dynamic-slice
  111.6 1.3 dynamic-update-slice.1
  112.9 1.3 dynamic-update-slice
  114.2 5.1 %all-reduce.4 = (f32[2]{0:T(128)S(1)}, f32[2]{0:T(128)S(1)}) all-reduce(f32[2]{0:T(128)S(1)} %dynamic-update-slice.1, f32[2]{0:T(128)S(1)} %dynamic-update-slice), channel_id=1, replica_groups=mesh['groups'=2,'zone'=4,'scen'=2,'hour'=2] {'scen'}, use_global_device_ids=true, to_apply=%add.1 | all-reduce | flops 4 | bytes 32
  119.3 0.6 fusion.100
  122.5 0.6 fusion.99
  125.1 0.0 copy-start.6
  125.1 0.0 copy-start.9
  125.1 0.0 slice-start
  125.1 8.3 %fusion.72 = f32[64,1024]{1,0:T(8,128)S(1)} fusion(bf16[256,8,64]{0,2,1:T(8,128)(2,1)S(1)} %copy.35, f32[8,1024,256]{2,1,0:T(8,128)} %get-tuple-element.44, f32[256]{0:T(256)S(1)} %exponential_divide_fusion, f32[8,1024]{1,0:T(8,128)S(1)} %get-tuple-element.35, f32[8,1024]{1,0:T(8,128)S(1)} %get-tuple-element.52, f32[8,1024]{1,0:T(8,128)S(1)} %get-tuple-element.29, ...), kind=kOutput, calls=%fused_computation.97 | convolution fusion | flops 295108608 | bytes 10060800 | tf_op jit(solution)/shard_map/shp,hsz->hpz/dot_general | solution.py:90
  133.5 0.0 copy-done.6
  133.5 0.0 copy-done.9
  133.5 0.0 slice-start.1
  133.5 6.3 %fusion.74 = f32[64,1024]{1,0:T(8,128)S(1)} fusion(bf16[256,8,64]{0,2,1:T(8,128)(2,1)S(1)} %copy.33, f32[8,1024,256]{2,1,0:T(8,128)S(1)} %copy-done.9, f32[256]{0:T(256)S(1)} %exponential_divide_fusion, f32[8,1024]{1,0:T(8,128)S(1)} %get-tuple-element.36, f32[8,1024]{1,0:T(8,128)S(1)} %get-tuple-element.51, f32[8,1024]{1,0:T(8,128)S(1)} %get-tuple-element.30, ...), kind=kOutput, calls=%fused_computation.101 | convolution fusion | flops 295108608 | bytes 10060800 | tf_op jit(solution)/shard_map/shp,hsz->hpz/dot_general | solution.py:90
  139.8 0.0 slice-done
  139.8 0.0 slice-done.1
  139.9 0.0 copy-start.7
  139.9 6.3 %fusion.73 = f32[64,1024]{1,0:T(8,128)S(1)} fusion(bf16[256,8,64]{0,2,1:T(8,128)(2,1)S(1)} %copy.34, f32[8,1024,256]{2,1,0:T(8,128)S(1)} %bitcast.233, f32[256]{0:T(256)S(1)} %exponential_divide_fusion, f32[8,1024]{1,0:T(8,128)S(1)} %get-tuple-element.34, f32[8,1024]{1,0:T(8,128)S(1)} %get-tuple-element.53, f32[8,1024]{1,0:T(8,128)S(1)} %get-tuple-element.28, ...), kind=kOutput, calls=%fused_computation.99 | convolution fusion | flops 295108608 | bytes 10060800 | tf_op jit(solution)/shard_map/shp,hsz->hpz/dot_general | solution.py:90
  146.2 0.6 convolution_multiply_fusion
  146.8 57.6 %all-reduce.2 = f32[64,64]{1,0:T(8,128)S(1)} all-reduce(f32[64,64]{1,0:T(8,128)S(1)} %convolution_multiply_fusion), channel_id=2, replica_groups=mesh['groups'=2,'zone'=4,'scen'=2,'hour'=2] {'zone','scen','hour'}, use_global_device_ids=true, to_apply=%region_12.13.clone | all-reduce | flops 4096 | bytes 32768
  204.4 0.0 copy-done.7
  204.4 0.6 dynamic-slice.2
  205.7 0.6 constant_dynamic-slice_fusion
  (11 shorter events, 0.1 us)
Async XLA Ops:
  0.6 45.3 %copy-start = (f32[64,64]{1,0:T(8,128)S(1)}, f32[64,64]{1,0:T(8,128)}, u32[]{:S(2)}) copy-start(f32[64,64]{1,0:T(8,128)} %param.9) | copy-start | bytes 49156
  0.6 40.5 %copy-start.3 = (f32[1024]{0:T(1024)S(1)}, f32[1024]{0:T(1024)}, u32[]{:S(2)}) copy-start(f32[1024]{0:T(1024)} %param.13) | copy-start | bytes 12292
  0.7 40.6 %copy-start.2 = (s32[24,1024]{1,0:T(8,128)S(1)}, s32[24,1024]{1,0:T(8,128)}, u32[]{:S(2)}) copy-start(s32[24,1024]{1,0:T(8,128)} %param.12) | copy-start | bytes 294916
  0.7 40.6 %copy-start.4 = (s32[1024]{0:T(1024)S(1)}, s32[1024]{0:T(1024)}, u32[]{:S(2)}) copy-start(s32[1024]{0:T(1024)} %param.10) | copy-start | bytes 12292
  0.7 40.7 %copy-start.1 = (s32[1024]{0:T(1024)S(1)}, s32[1024]{0:T(1024)}, u32[]{:S(2)}) copy-start(s32[1024]{0:T(1024)} %param.11) | copy-start | bytes 12292
  2.9 4.9 %all-to-all-start = ((bf16[2,2,24576]{2,1,0:T(2,128)(2,1)}), bf16[2,2,24576]{2,1,0:T(2,128)(2,1)S(1)}, u32[]{:S(2)}, u32[]{:S(2)}) async-start(bf16[2,2,24576]{2,1,0:T(2,128)(2,1)} %reshape.77), calls=%async_computation | async-start | bytes 393216 | tf_op jit(solution)/shard_map/all_to_all | solution.py:41
  51.7 13.8 %copy-start.5 = (bf16[24,64,1024]{2,1,0:T(8,128)(2,1)S(1)}, bf16[24,64,1024]{2,1,0:T(8,128)(2,1)}, u32[]{:S(2)}) copy-start(bf16[24,64,1024]{2,1,0:T(8,128)(2,1)} %param.8) | copy-start | bytes 9437188
  78.8 32.3 %copy-start.8 = (u32[32]{0:T(128)S(1)}, u32[32]{0:T(128)}, u32[]{:S(2)}) copy-start(u32[32]{0:T(128)} %constant.81) | copy-start | bytes 388
  125.1 8.4 %copy-start.6 = (bf16[24,64,1024]{2,1,0:T(8,128)(2,1)S(1)}, bf16[24,64,1024]{2,1,0:T(8,128)(2,1)}, u32[]{:S(2)}) copy-start(bf16[24,64,1024]{2,1,0:T(8,128)(2,1)} %param.8) | copy-start | bytes 9437188
  125.1 8.3 %copy-start.9 = (f32[8,1024,256]{2,1,0:T(8,128)S(1)}, f32[8,1024,256]{2,1,0:T(8,128)}, u32[]{:S(2)}) copy-start(f32[8,1024,256]{2,1,0:T(8,128)} %get-tuple-element.46) | copy-start | bytes 25165828
  125.1 14.7 %slice-start = ((s8[8388608]{0:T(1024)(128)(4,1)}), s8[4194304]{0:T(1024)(128)(4,1)S(1)}, s32[]{:S(2)}) async-start(s8[8388608]{0:T(1024)(128)(4,1)} %bitcast.232), calls=%async_computation.1 | async-start | bytes 8388608
  133.5 6.4 %slice-start.1 = ((s8[8388608]{0:T(1024)(128)(4,1)}), s8[4194304]{0:T(1024)(128)(4,1)S(1)}, s32[]{:S(2)}) async-start(s8[8388608]{0:T(1024)(128)(4,1)} %bitcast.232), calls=%async_computation.2 | async-start | bytes 8388608
  139.9 64.6 %copy-start.7 = (u32[32]{0:T(128)S(1)}, u32[32]{0:T(128)}, u32[]{:S(2)}) copy-start(u32[32]{0:T(128)} %constant.93) | copy-start | bytes 388
where the time goes:
time: 208 us; the launch traced here: 207 us
  blocking collectives  111 us (53%)
  matrix products  61.8 us (30%)
  local copies, waits for them, and re-layouts  17 us (8%)
  between operations  8.65 us (4%)
  other arithmetic  4.05 us (2%)
  starting transfers between devices  3.43 us (2%)
    unnamed x2, blocking collectives  62.7 us
    dot_general x3, matrix products, inside_climate_state(): jnp.einsum('shp,hpz->hsz', record_elements, coeff[initial_clock_time:init...  40.3 us
    all_gather x1, blocking collectives, on_device(): outlook_records = lax.all_gather(mine, 'zone', axis=0, tiled=True)  31.7 us
    dot_general x3, matrix products, on_device(): jnp.einsum('shp,hsz->hpz', record_elements, adjoint, preferred_element_ty...  20.9 us
    psum x1, blocking collectives, on_device(): loss_sum, weight_total = lax.psum((sums, weight_part), ('zone', 'hour'))  16.5 us
    unnamed x37, local copies, waits for them, and re-layouts  7.84 us
    gather x1, local copies, waits for them, and re-layouts, on_device(): candidate_plan = jnp.take(owner_ids, building_map)  4.53 us
  transfers between devices with their start and end apart: 1, of which 1 were waited for; matrix products, arithmetic and copies ran while one was open for 0% of the time, Pallas kernels for 0%

commit v1 on v0

--- a/solution.py
+++ b/solution.py
@@ -5,6 +5,12 @@
 from jax.sharding import PartitionSpec as P
 
 SHARPNESS = 200.0
+
+
+def swap_blocks(value, name, split, join):
+    pieces = jnp.split(value, lax.axis_size(name), axis=split)
+    arrived = lax.all_to_all(jnp.stack(pieces), name, 0, 0)
+    return jnp.concatenate(arrived, axis=join)
 
 
 def joined(value, axis, join):
@@ -38,7 +44,7 @@
     band_high = band_low + 1.0
     zone_weight = occupant_level[:, None] * floor_area[None, :]
     block_count = hour_local // 8
-    mine = lax.all_to_all(forcing, "hour", split_axis=1, concat_axis=0, tiled=True)
+    mine = swap_blocks(forcing, "hour", 1, 0)
 
     def inside_climate_state(outlook_records, initial_clock_time):
         record_elements = lax.slice_in_dim(

time: 208 us -> 233 us (1.12)
  other arithmetic: 4.05 us -> 43.3 us
  matrix products: 61.8 us -> 34.8 us
  local copies, waits for them, and re-layouts: 17 us -> 29.4 us
    reduce_sum x0 -> x3, other arithmetic: none -> 33 us  [on_device(): jnp.sum(penalty * zone_weight[initial_clock_time:initial_clock_time + 8][...]
    dot_general x3, matrix products: 40.3 us -> 13.7 us  [inside_climate_state(): jnp.einsum('shp,hpz->hsz', record_elements, coeff[initial_clock_time:init...]
    unnamed x37 -> x78, local copies, waits for them, and re-layouts: 7.84 us -> 14 us
    convert_element_type x0 -> x1, other arithmetic: none -> 2.69 us  [on_device(): (response.astype(jnp.float32) * zone_parameters.T[None, :, :]).astype(jnp...]
  transfers between devices with their start and end apart: 1 -> 1, of which waited for: 1 -> 0; matrix products, arithmetic and copies ran while one was open for 0% -> 1% of each run, Pallas kernels for 0% -> 0%
where the time goes in v1:
time: 233 us; the launch traced here: 232 us
  blocking collectives  112 us (48%)
  other arithmetic  43.3 us (19%)
  matrix products  34.8 us (15%)
  local copies, waits for them, and re-layouts  29.4 us (13%)
  between operations  9 us (4%)
  starting transfers between devices  3.43 us (1%)
    unnamed x2, blocking collectives  62.7 us
    reduce_sum x3, other arithmetic, on_device(): jnp.sum(penalty * zone_weight[initial_clock_time:initial_clock_time + 8][...  33 us
    all_gather x1, blocking collectives, on_device(): outlook_records = lax.all_gather(mine, 'zone', axis=0, tiled=True)  31.8 us
    dot_general x3, matrix products, on_device(): jnp.einsum('shp,hsz->hpz', record_elements, adjoint, preferred_element_ty...  19.4 us
    psum x1, blocking collectives, on_device(): loss_sum, weight_total = lax.psum((sums, weight_part), ('zone', 'hour'))  17.4 us
    unnamed x78, local copies, waits for them, and re-layouts  14 us
    dot_general x3, matrix products, inside_climate_state(): jnp.einsum('shp,hpz->hsz', record_elements, coeff[initial_clock_time:init...  13.7 us
  transfers between devices with their start and end apart: 1, of which 0 were waited for; matrix products, arithmetic and copies ran while one was open for 1% of the time, Pallas kernels for 0%

profile of v1, /device:TPU:0, one launch (start us, length us, event | category | flops | bytes accessed | tf_op | source)
XLA Modules:
  0.0 231.8 jit_solution(18109823604304292025)
XLA Ops:
  0.6 0.0 copy-start
  0.7 1.1 slice_bitcast_fusion.1
  1.8 0.1 pad_maximum_fusion
  1.8 1.0 reshape.81
  2.8 3.4 %all-to-all-start = ((bf16[2,2,24576]{2,1,0:T(2,128)(2,1)}), bf16[2,2,24576]{2,1,0:T(2,128)(2,1)S(1)}, u32[]{:S(2)}, u32[]{:S(2)}) async-start(bf16[2,2,24576]{2,1,0:T(2,128)(2,1)} %reshape.81), calls=%async_computation | async-start | bytes 393216 | tf_op jit(solution)/shard_map/all_to_all | solution.py:12
  6.3 1.5 fusion.21
  7.8 0.0 all-to-all-done
  7.8 0.3 reshape.82
  8.1 0.0 copy-start.22
  8.1 31.8 %all_gather.16 = bf16[256,24,64]{2,1,0:T(8,128)(2,1)S(1)} all-gather(bf16[64,24,64]{2,1,0:T(8,128)(2,1)S(1)} %bitcast.22), channel_id=1, replica_groups=mesh['groups'=2,'zone'=4,'scen'=2,'hour'=2] {'zone'}, dimensions={0}, use_global_device_ids=true | all-gather | bytes 983040 | tf_op jit(solution)/shard_map/all_gather | solution.py:84
  40.0 1.2 fusion.29
  41.2 2.3 copy.18
  43.5 0.0 copy-done.1
  43.5 4.5 %gather_fusion = s32[1024]{0:T(1024)S(1)} fusion(s32[1024]{0:T(1024)S(1)} %copy-done.1, s32[1024]{0:T(1024)S(1)} %fusion.22), kind=kCustom, calls=%fused_computation | custom fusion | bytes 12288 | tf_op jit(solution)/shard_map/jit(_take)/gather | solution.py:40
  48.1 4.0 %gather_fusion.1 = f32[1024,64]{1,0:T(8,128)} fusion(f32[64,64]{1,0:T(8,128)S(1)} %copy-done, s32[1024]{0:T(1024)S(1)} %fusion.23), kind=kCustom, calls=%fused_computation.1 | custom fusion | bytes 528384 | tf_op jit(solution)/shard_map/jit(_take)/gather | solution.py:41
  52.1 2.1 select_bitcast_fusion
  54.2 1.2 copy.14
  55.4 0.6 multiply_add_fusion
  56.0 0.1 broadcast_multiply_fusion
  56.1 0.6 fusion.32
  56.7 2.0 copy.17
  58.8 2.0 copy.19
  60.8 0.6 reduce_sum.84
  61.4 1.5 fusion.30
  62.8 0.0 copy-done.2
  62.9 2.7 %multiply_convert_fusion.3 = bf16[24,64,1024]{2,1,0:T(8,128)(2,1)} fusion(bf16[24,64,1024]{2,1,0:T(8,128)(2,1)S(1)} %copy-done.2, f32[64,1024]{1,0:T(8,128)S(1)} %copy.14), kind=kLoop, calls=%fused_computation.21 | loop fusion | flops 4718592 | bytes 6553600 | tf_op jit(solution)/shard_map/convert_element_type | solution.py:42
  66.9 4.9 %fusion.5 = (u8[256,1024]{1,0:T(8,128)(4,1)S(1)}, u8[256,1024]{1,0:T(8,128)(4,1)S(1)}, f32[8,256,1024]{2,1,0:T(8,128)S(1)}) fusion(f32[8,1024]{1,0:T(8,128)} %get-tuple-element.36, f32[8,1024]{1,0:T(8,128)} %get-tuple-element.56, bf16[256,8,64]{0,2,1:T(8,128)(2,1)} %copy.18, bf16[24,64,1024]{2,1,0:T(8,128)(2,1)} %multiply_convert_fusion.3), kind=kOutput, calls=%fused_computation.30 | convolution fusion | flops 293076992 | bytes 10289152 | tf_op jit(solution)/shard_map/shp,hpz->hsz/dot_general | solution.py:53
  71.8 0.0 copy-start.30
  71.8 0.0 copy-done.3
  71.8 0.0 copy-done.7
  71.8 0.0 copy-done.12
  71.9 0.0 copy-done.13
  71.9 0.0 copy-start.5
  71.9 0.0 copy-start.10
  71.9 0.0 copy-start.11
  71.9 4.4 %fusion.3 = (u8[256,1024]{1,0:T(8,128)(4,1)S(1)}, u8[256,1024]{1,0:T(8,128)(4,1)S(1)}, f32[8,256,1024]{2,1,0:T(8,128)S(1)}) fusion(f32[8,1024]{1,0:T(8,128)S(1)} %copy-done.12, f32[8,1024]{1,0:T(8,128)S(1)} %copy-done.13, bf16[256,8,64]{0,2,1:T(8,128)(2,1)S(1)} %copy-done.7, bf16[24,64,1024]{2,1,0:T(8,128)(2,1)S(1)} %copy-done.3), kind=kOutput, calls=%fused_computation.28 | convolution fusion | flops 293076992 | bytes 10289152 | tf_op jit(solution)/shard_map/shp,hpz->hsz/dot_general | solution.py:53
  76.4 4.4 %fusion.7 = (u8[256,1024]{1,0:T(8,128)(4,1)S(1)}, u8[256,1024]{1,0:T(8,128)(4,1)S(1)}, f32[8,256,1024]{2,1,0:T(8,128)S(1)}) fusion(f32[8,1024]{1,0:T(8,128)S(1)} %copy-done.10, f32[8,1024]{1,0:T(8,128)S(1)} %copy-done.11, bf16[256,8,64]{0,2,1:T(8,128)(2,1)S(1)} %copy-done.5, bf16[24,64,1024]{2,1,0:T(8,128)(2,1)S(1)} %copy-done.3), kind=kOutput, calls=%fused_computation.32 | convolution fusion | flops 293076992 | bytes 10289152 | tf_op jit(solution)/shard_map/shp,hpz->hsz/dot_general | solution.py:53
  80.9 11.0 %multiply_reduce_fusion.1 = f32[256]{0:T(256)S(1)} fusion(f32[8,256,1024]{2,1,0:T(8,128)S(1)} %get-tuple-element.53, f32[8,1024]{1,0:T(8,128)S(1)} %copy-done.21, f32[8,1024]{1,0:T(8,128)S(1)} %copy-done.16, f32[8,1024]{1,0:T(8,128)S(1)} %copy-done.15, u8[256,1024]{1,0:T(8,128)(4,1)S(1)} %get-tuple-element.13, u8[256,1024]{1,0:T(8,128)(4,1)S(1)} %get-tuple-element.12), kind=kLoop, calls=%fused_computation.19 | loop fusion | flops 46137088 | bytes 9012224 | tf_op jit(solution)/shard_map/reduce_sum | solution.py:70
  91.9 10.8 %multiply_reduce_fusion.2 = f32[256]{0:T(256)S(1)} fusion(f32[8,256,1024]{2,1,0:T(8,128)S(1)} %get-tuple-element.52, f32[8,1024]{1,0:T(8,128)S(1)} %copy-done.19, f32[8,1024]{1,0:T(8,128)S(1)} %copy-done.13, f32[8,1024]{1,0:T(8,128)S(1)} %copy-done.12, u8[256,1024]{1,0:T(8,128)(4,1)S(1)} %get-tuple-element.20, u8[256,1024]{1,0:T(8,128)(4,1)S(1)} %get-tuple-element.14), kind=kLoop, calls=%fused_computation.20 | loop fusion | flops 46137088 | bytes 9012224 | tf_op jit(solution)/shard_map/reduce_sum | solution.py:70
  102.7 0.0 copy-start.25
  102.8 11.2 %multiply_reduce_fusion = f32[256]{0:T(256)S(1)} fusion(f32[8,256,1024]{2,1,0:T(8,128)S(1)} %get-tuple-element.51, f32[8,1024]{1,0:T(8,128)S(1)} %copy-done.17, f32[8,1024]{1,0:T(8,128)S(1)} %copy-done.11, f32[8,1024]{1,0:T(8,128)S(1)} %copy-done.10, u8[256,1024]{1,0:T(8,128)(4,1)S(1)} %get-tuple-element.22, u8[256,1024]{1,0:T(8,128)(4,1)S(1)} %get-tuple-element.21), kind=kLoop, calls=%fused_computation.18 | loop fusion | flops 46137088 | bytes 9012224 | tf_op jit(solution)/shard_map/reduce_sum | solution.py:70
  113.9 17.4 %all-reduce.3 = (f32[256]{0:T(256)S(1)}, f32[]{:T(128)}) all-reduce(f32[256]{0:T(256)S(1)} %add_add_fusion, f32[]{:T(128)S(6)} %mul.142), channel_id=1, replica_groups=mesh['groups'=2,'zone'=4,'scen'=2,'hour'=2] {'zone','hour'}, use_global_device_ids=true, to_apply=%region_3.4 | all-reduce | flops 257 | bytes 2056 | tf_op jit(solution)/shard_map/psum | solution.py:74
  131.3 1.2 fusion.28
  132.6 0.6 dynamic-slice
  133.2 1.3 exponential_reduce_fusion
  134.5 1.4 dynamic-update-slice
  135.9 0.5 broadcast.77.clone
  136.4 0.0 copy-done.26
  136.5 2.5 %dynamic-update-slice.1 = f32[2]{0:T(128)} dynamic-update-slice(f32[2]{0:T(128)} %broadcast.77.clone, f32[1]{0:T(128)} %bitcast.8, u32[]{:T(128)} %bitcast.5) | dynamic-update-slice | bytes 12
  139.0 5.0 %all-reduce.4 = (f32[2]{0:T(128)S(1)}, f32[2]{0:T(128)S(1)}) all-reduce(f32[2]{0:T(128)} %dynamic-update-slice.1, f32[2]{0:T(128)} %copy-done.26), channel_id=1, replica_groups=mesh['groups'=2,'zone'=4,'scen'=2,'hour'=2] {'scen'}, use_global_device_ids=true, to_apply=%add.1 | all-reduce | flops 4 | bytes 32
  144.0 0.6 fusion.34
  147.3 0.6 fusion.33
  150.0 0.0 slice-start
  150.0 8.2 %multiply_reduce_fusion.4 = f32[64,1024]{1,0:T(8,128)} fusion(bf16[256,8,64]{0,2,1:T(8,128)(2,1)S(1)} %copy-done.4, f32[8,256,1024]{2,1,0:T(8,128)} %copy-done.30, f32[256]{0:T(256)S(1)} %exponential_divide_fusion, f32[8,1024]{1,0:T(8,128)} %get-tuple-element.42, f32[8,1024]{1,0:T(8,128)} %get-tuple-element.56, f32[8,1024]{1,0:T(8,128)} %get-tuple-element.36, ...), kind=kOutput, calls=%fused_computation.26 | convolution fusion | flops 295108608 | bytes 10060800 | tf_op jit(solution)/shard_map/shp,hsz->hpz/dot_general | solution.py:96
  158.2 0.0 copy-done.20
  158.3 0.0 slice-start.1
  158.3 5.6 %multiply_reduce_fusion.5 = f32[64,1024]{1,0:T(8,128)} fusion(bf16[256,8,64]{0,2,1:T(8,128)(2,1)S(1)} %copy-done.8, f32[8,256,1024]{2,1,0:T(8,128)S(1)} %copy-done.29, f32[256]{0:T(256)S(1)} %exponential_divide_fusion, f32[8,1024]{1,0:T(8,128)S(1)} %copy-done.20, f32[8,1024]{1,0:T(8,128)S(1)} %copy-done.14, f32[8,1024]{1,0:T(8,128)S(1)} %copy-done.12, ...), kind=kOutput, calls=%fused_computation.27 | convolution fusion | flops 295108608 | bytes 10060800 | tf_op jit(solution)/shard_map/shp,hsz->hpz/dot_general | solution.py:96
  163.9 0.0 copy-done.18
  163.9 0.0 copy-start.24
  163.9 5.6 %multiply_reduce_fusion.3 = f32[64,1024]{1,0:T(8,128)} fusion(bf16[256,8,64]{0,2,1:T(8,128)(2,1)S(1)} %copy-done.6, f32[8,256,1024]{2,1,0:T(8,128)S(1)} %bitcast.24, f32[256]{0:T(256)S(1)} %exponential_divide_fusion, f32[8,1024]{1,0:T(8,128)S(1)} %copy-done.18, f32[8,1024]{1,0:T(8,128)S(1)} %copy-done.11, f32[8,1024]{1,0:T(8,128)S(1)} %copy-done.10, ...), kind=kOutput, calls=%fused_computation.25 | convolution fusion | flops 295108608 | bytes 10060800 | tf_op jit(solution)/shard_map/shp,hsz->hpz/dot_general | solution.py:96
  169.5 1.6 convolution_multiply_fusion
  171.2 57.6 %all-reduce.2 = f32[64,64]{1,0:T(8,128)S(1)} all-reduce(f32[64,64]{1,0:T(8,128)S(1)} %convolution_multiply_fusion), channel_id=2, replica_groups=mesh['groups'=2,'zone'=4,'scen'=2,'hour'=2] {'zone','scen','hour'}, use_global_device_ids=true, to_apply=%region_12.13.clone | all-reduce | flops 4096 | bytes 32768
  228.8 0.6 dynamic-slice.2
  230.0 0.6 constant_dynamic-slice_fusion
  (54 shorter events, 0.1 us)
Async XLA Ops:
  0.6 47.5 %copy-start = (f32[64,64]{1,0:T(8,128)S(1)}, f32[64,64]{1,0:T(8,128)}, u32[]{:S(2)}) copy-start(f32[64,64]{1,0:T(8,128)} %param.9) | copy-start | bytes 49156
  0.6 42.9 %copy-start.23 = (s32[1024]{0:T(1024)S(1)}, s32[1024]{0:T(1024)}, u32[]{:S(2)}) copy-start(s32[1024]{0:T(1024)} %param.10) | copy-start | bytes 12292
  0.7 42.9 %copy-start.1 = (s32[1024]{0:T(1024)S(1)}, s32[1024]{0:T(1024)}, u32[]{:S(2)}) copy-start(s32[1024]{0:T(1024)} %param.11) | copy-start | bytes 12292
  2.8 5.0 %all-to-all-start = ((bf16[2,2,24576]{2,1,0:T(2,128)(2,1)}), bf16[2,2,24576]{2,1,0:T(2,128)(2,1)S(1)}, u32[]{:S(2)}, u32[]{:S(2)}) async-start(bf16[2,2,24576]{2,1,0:T(2,128)(2,1)} %reshape.81), calls=%async_computation | async-start | bytes 393216 | tf_op jit(solution)/shard_map/all_to_all | solution.py:12
  8.1 47.9 %copy-start.22 = (f32[1024]{0:T(1024)S(1)}, f32[1024]{0:T(1024)}, u32[]{:S(2)}) copy-start(f32[1024]{0:T(1024)} %param.13) | copy-start | bytes 12292
  40.0 22.9 %copy-start.2 = (bf16[24,64,1024]{2,1,0:T(8,128)(2,1)S(1)}, bf16[24,64,1024]{2,1,0:T(8,128)(2,1)}, u32[]{:S(2)}) copy-start(bf16[24,64,1024]{2,1,0:T(8,128)(2,1)} %param.8) | copy-start | bytes 9437188
  66.8 5.0 %copy-start.3 = (bf16[24,64,1024]{2,1,0:T(8,128)(2,1)S(1)}, bf16[24,64,1024]{2,1,0:T(8,128)(2,1)}, u32[]{:S(2)}) copy-start(bf16[24,64,1024]{2,1,0:T(8,128)(2,1)} %multiply_convert_fusion.3) | copy-start | bytes 9437188
  66.9 5.0 %copy-start.7 = (bf16[256,8,64]{0,2,1:T(8,128)(2,1)S(1)}, bf16[256,8,64]{0,2,1:T(8,128)(2,1)}, u32[]{:S(2)}) copy-start(bf16[256,8,64]{0,2,1:T(8,128)(2,1)} %copy.17) | copy-start | bytes 786436
  66.9 5.0 %copy-start.12 = (f32[8,1024]{1,0:T(8,128)S(1)}, f32[8,1024]{1,0:T(8,128)}, u32[]{:S(2)}) copy-start(f32[8,1024]{1,0:T(8,128)} %get-tuple-element.38) | copy-start | bytes 98308
  66.9 5.0 %copy-start.13 = (f32[8,1024]{1,0:T(8,128)S(1)}, f32[8,1024]{1,0:T(8,128)}, u32[]{:S(2)}) copy-start(f32[8,1024]{1,0:T(8,128)} %get-tuple-element.54) | copy-start | bytes 98308
  71.8 9.0 %copy-start.30 = (f32[8,256,1024]{2,1,0:T(8,128)}, f32[8,256,1024]{2,1,0:T(8,128)S(1)}, u32[]{:S(2)}) copy-start(f32[8,256,1024]{2,1,0:T(8,128)S(1)} %get-tuple-element.53) | copy-start | bytes 25165828
  71.9 4.5 %copy-start.5 = (bf16[256,8,64]{0,2,1:T(8,128)(2,1)S(1)}, bf16[256,8,64]{0,2,1:T(8,128)(2,1)}, u32[]{:S(2)}) copy-start(bf16[256,8,64]{0,2,1:T(8,128)(2,1)} %copy.19) | copy-start | bytes 786436
  71.9 4.5 %copy-start.10 = (f32[8,1024]{1,0:T(8,128)S(1)}, f32[8,1024]{1,0:T(8,128)}, u32[]{:S(2)}) copy-start(f32[8,1024]{1,0:T(8,128)} %get-tuple-element.37) | copy-start | bytes 98308
  71.9 4.5 %copy-start.11 = (f32[8,1024]{1,0:T(8,128)S(1)}, f32[8,1024]{1,0:T(8,128)}, u32[]{:S(2)}) copy-start(f32[8,1024]{1,0:T(8,128)} %get-tuple-element.55) | copy-start | bytes 98308
  76.3 15.6 %copy-start.28 = (f32[8,256,1024]{2,1,0:T(8,128)}, f32[8,256,1024]{2,1,0:T(8,128)S(1)}, u32[]{:S(2)}) copy-start(f32[8,256,1024]{2,1,0:T(8,128)S(1)} %get-tuple-element.52) | copy-start | bytes 25165828
  76.3 4.5 %copy-start.15 = (f32[8,1024]{1,0:T(8,128)S(1)}, f32[8,1024]{1,0:T(8,128)}, u32[]{:S(2)}) copy-start(f32[8,1024]{1,0:T(8,128)} %get-tuple-element.36) | copy-start | bytes 98308
  76.4 4.5 %copy-start.16 = (f32[8,1024]{1,0:T(8,128)S(1)}, f32[8,1024]{1,0:T(8,128)}, u32[]{:S(2)}) copy-start(f32[8,1024]{1,0:T(8,128)} %get-tuple-element.56) | copy-start | bytes 98308
  76.4 4.5 %copy-start.21 = (f32[8,1024]{1,0:T(8,128)S(1)}, f32[8,1024]{1,0:T(8,128)}, u32[]{:S(2)}) copy-start(f32[8,1024]{1,0:T(8,128)} %get-tuple-element.42) | copy-start | bytes 98308
  80.8 22.0 %copy-start.27 = (f32[8,256,1024]{2,1,0:T(8,128)}, f32[8,256,1024]{2,1,0:T(8,128)S(1)}, u32[]{:S(2)}) copy-start(f32[8,256,1024]{2,1,0:T(8,128)S(1)} %get-tuple-element.51) | copy-start | bytes 25165828
  80.8 11.1 %copy-start.19 = (f32[8,1024]{1,0:T(8,128)S(1)}, f32[8,1024]{1,0:T(8,128)}, u32[]{:S(2)}) copy-start(f32[8,1024]{1,0:T(8,128)} %get-tuple-element.44) | copy-start | bytes 98308
  91.9 10.9 %copy-start.17 = (f32[8,1024]{1,0:T(8,128)S(1)}, f32[8,1024]{1,0:T(8,128)}, u32[]{:S(2)}) copy-start(f32[8,1024]{1,0:T(8,128)} %get-tuple-element.43) | copy-start | bytes 98308
  102.7 29.9 %copy-start.25 = (u32[32]{0:T(128)S(1)}, u32[32]{0:T(128)}, u32[]{:S(2)}) copy-start(u32[32]{0:T(128)} %constant.81) | copy-start | bytes 388
  102.7 47.2 %copy-start.4 = (bf16[256,8,64]{0,2,1:T(8,128)(2,1)S(1)}, bf16[256,8,64]{0,2,1:T(8,128)(2,1)}, u32[]{:S(2)}) copy-start(bf16[256,8,64]{0,2,1:T(8,128)(2,1)} %copy.18) | copy-start | bytes 786436
  135.9 0.6 copy-start.26
  150.0 8.3 %copy-start.8 = (bf16[256,8,64]{0,2,1:T(8,128)(2,1)S(1)}, bf16[256,8,64]{0,2,1:T(8,128)(2,1)}, u32[]{:S(2)}) copy-start(bf16[256,8,64]{0,2,1:T(8,128)(2,1)} %copy.17) | copy-start | bytes 786436
  150.0 8.2 %copy-start.14 = (f32[8,1024]{1,0:T(8,128)S(1)}, f32[8,1024]{1,0:T(8,128)}, u32[]{:S(2)}) copy-start(f32[8,1024]{1,0:T(8,128)} %get-tuple-element.54) | copy-start | bytes 98308
  150.0 8.2 %copy-start.20 = (f32[8,1024]{1,0:T(8,128)S(1)}, f32[8,1024]{1,0:T(8,128)}, u32[]{:S(2)}) copy-start(f32[8,1024]{1,0:T(8,128)} %get-tuple-element.44) | copy-start | bytes 98308
  150.0 8.2 %copy-start.29 = (f32[8,256,1024]{2,1,0:T(8,128)S(1)}, f32[8,256,1024]{2,1,0:T(8,128)}, u32[]{:S(2)}) copy-start(f32[8,256,1024]{2,1,0:T(8,128)} %copy-done.28) | copy-start | bytes 25165828
  150.0 13.9 %slice-start = ((s8[8388608]{0:T(1024)(128)(4,1)}), s8[4194304]{0:T(1024)(128)(4,1)S(1)}, s32[]{:S(2)}) async-start(s8[8388608]{0:T(1024)(128)(4,1)} %bitcast.23), calls=%async_computation.1 | async-start | bytes 8388608
  158.2 5.7 %copy-start.6 = (bf16[256,8,64]{0,2,1:T(8,128)(2,1)S(1)}, bf16[256,8,64]{0,2,1:T(8,128)(2,1)}, u32[]{:S(2)}) copy-start(bf16[256,8,64]{0,2,1:T(8,128)(2,1)} %copy.19) | copy-start | bytes 786436
  158.3 5.6 %copy-start.18 = (f32[8,1024]{1,0:T(8,128)S(1)}, f32[8,1024]{1,0:T(8,128)}, u32[]{:S(2)}) copy-start(f32[8,1024]{1,0:T(8,128)} %get-tuple-element.43) | copy-start | bytes 98308
  158.3 5.6 %slice-start.1 = ((s8[8388608]{0:T(1024)(128)(4,1)}), s8[4194304]{0:T(1024)(128)(4,1)S(1)}, s32[]{:S(2)}) async-start(s8[8388608]{0:T(1024)(128)(4,1)} %bitcast.23), calls=%async_computation.2 | async-start | bytes 8388608
  163.9 5.6 %copy-start.9 = (f32[64,1024]{1,0:T(8,128)S(1)}, f32[64,1024]{1,0:T(8,128)}, u32[]{:S(2)}) copy-start(f32[64,1024]{1,0:T(8,128)} %multiply_reduce_fusion.4) | copy-start | bytes 786436
  163.9 64.9 %copy-start.24 = (u32[32]{0:T(128)S(1)}, u32[32]{0:T(128)}, u32[]{:S(2)}) copy-start(u32[32]{0:T(128)} %constant.93) | copy-start | bytes 388
